TPU v7x, 32 devices: a whole 2x2x4 slice. The times are simulated.
32 devices in a mesh: groups: 2 (over x), row: 16 (over z, y, core).
Axes of the slice: x: 2, y: 2, z: 4, core: 2. Of those that a mesh axis runs over, the one named last changes fastest.
Arguments:
- pair: bfloat16 [512, 256, 128], P(('groups', 'row')), parts along dimension 0, may hold values from -6 to 6
- residue_mask: int32 [512], P('groups'), parts along dimension 0, may hold values 0 or 1
- ln_in_gain: float32 [128], replicated, may hold values from 0.1 to 1.9
- w_a_gate: bfloat16 [128, 128], replicated, may hold values from -0.5 to 0.5
- w_a_proj: bfloat16 [128, 128], replicated, may hold values from -0.5 to 0.5
- w_b_gate: bfloat16 [128, 128], replicated, may hold values from -0.5 to 0.5
- w_b_proj: bfloat16 [128, 128], replicated, may hold values from -0.5 to 0.5
- w_out_gate: bfloat16 [128, 128], replicated, may hold values from -0.5 to 0.5
- ln_out_gain: float32 [128], replicated, may hold values from 0.1 to 1.9
- w_out: bfloat16 [128, 128], replicated, may hold values from -0.5 to 0.5
Outputs:
- pair_columns: bfloat16 [512, 256, 128], P('groups', 'row'), parts along dimension 0
There are 2 independent parts, one for each index of `groups`. A program takes and returns all parts, laid end to end along the dimension named above; an argument that names none is the same for every part. Nothing has to cross between parts.
Inputs may be any that keep to these rules, and one draw needn't show every extreme that they name: `residue_mask`: 256 flags, 1 for a resolved token.
All inputs are finite; a program needn't handle non-finite values.
Results may differ from a plain program's by a relative error of at most 0.002.
Values may be sent and summed in bfloat16 or wider, within the bound.
A program may use at most 128 MiB of HBM per device.

v0:
```python
import jax
import jax.numpy as jnp
from jax import lax
from jax.sharding import PartitionSpec as P

epsilon = 1e-05


def passed_along(block, axis, distance):
    devices = range(lax.axis_size(axis))
    route = [((i - distance) % len(devices), i) for i in devices]
    return lax.ppermute(block, axis, route)


def normalize(values, scale_gain):
    center = jnp.mean(values, axis=-1, keepdims=True)
    centered = values - center
    spread = jnp.mean(centered * centered, axis=-1, keepdims=True)
    return centered * lax.rsqrt(spread + epsilon) * scale_gain


def band_update(
    left_cols, right_cols, normed, column_block, rows_n, ln_out_gain, w_out_gate, w_out
):
    channels = normed.shape[2]
    product = jnp.einsum("cik,cjk->cij", left_cols, right_cols, preferred_element_type=jnp.float32)
    product = jnp.transpose(product, (1, 2, 0))
    normed_x = (
        normalize(product, ln_out_gain).astype(jnp.bfloat16).reshape(rows_n * rows_n, channels)
    )
    update = jnp.dot(normed_x, w_out, preferred_element_type=jnp.float32)
    columns = lax.dynamic_slice_in_dim(normed, column_block * rows_n, rows_n, 1).reshape(
        rows_n * rows_n, channels
    )
    gating = jax.nn.sigmoid(jnp.dot(columns, w_out_gate, preferred_element_type=jnp.float32))
    return (gating * update).reshape(rows_n, rows_n, channels)


def shards(
    pair,
    residue_mask,
    ln_in_gain,
    w_a_gate,
    w_a_proj,
    w_b_gate,
    w_b_proj,
    w_out_gate,
    ln_out_gain,
    w_out,
):
    rows_n, tokens, channels = pair.shape
    blocks = lax.axis_size("row")
    position = lax.axis_index("row")
    moved_pair = lax.all_to_all(pair, "row", split_axis=1, concat_axis=0, tiled=True)
    mask_float = residue_mask.astype(jnp.float32)
    row_mask = lax.dynamic_slice_in_dim(mask_float, position * rows_n, rows_n)
    pair_mask = (row_mask[:, None] * mask_float[None, :])[:, :, None]
    normed = normalize(pair.astype(jnp.float32), ln_in_gain).astype(jnp.bfloat16)
    weights = jnp.concatenate((w_a_gate, w_a_proj, w_b_gate, w_b_proj), axis=1)
    projected = jnp.dot(
        normed.reshape(rows_n * tokens, channels), weights, preferred_element_type=jnp.float32
    )
    projected = projected.reshape(rows_n, tokens, 4 * channels)
    left = (
        jax.nn.sigmoid(projected[:, :, :channels])
        * projected[:, :, channels : 2 * channels]
        * pair_mask
    )
    right = (
        jax.nn.sigmoid(projected[:, :, 2 * channels : 3 * channels])
        * projected[:, :, 3 * channels :]
        * pair_mask
    )
    left_cols = jnp.transpose(left.astype(jnp.bfloat16), (2, 0, 1))
    right_cols = jnp.transpose(right.astype(jnp.bfloat16), (2, 0, 1))
    arrived = [right_cols]
    current = right_cols
    for offset in range(2):
        current = passed_along(current, "row", 1)
        arrived.append(current)
    deltas = []
    for offset in range(3):
        column_block = (position - offset) % blocks
        deltas.append(
            band_update(
                left_cols,
                arrived[offset],
                normed,
                column_block,
                rows_n,
                ln_out_gain,
                w_out_gate,
                w_out,
            )
        )
    incoming = [
        deltas[0],
        passed_along(deltas[1].astype(jnp.bfloat16), "row", -1).astype(jnp.float32),
        passed_along(deltas[2].astype(jnp.bfloat16), "row", -2).astype(jnp.float32),
    ]
    columns_now = moved_pair
    for offset in range(3):
        start = (position + offset) % blocks * rows_n
        old_block = lax.dynamic_slice_in_dim(columns_now, start, rows_n, 0)
        new_block = (old_block.astype(jnp.float32) + incoming[offset]).astype(jnp.bfloat16)
        columns_now = lax.dynamic_update_slice_in_dim(columns_now, new_block, start, 0)
    return columns_now


def solution(mesh):
    placed = (P(("groups", "row"), None, None), P("groups"), P(), P(), P(), P(), P(), P(), P(), P())
    return jax.shard_map(
        shards, mesh=mesh, in_specs=placed, out_specs=P("groups", "row", None), check_vma=False
    )
```

profile of v0, /device:TPU:15, one launch (start us, length us, event | category | flops | bytes accessed | tf_op | source)
XLA Modules:
  0.0 72.8 jit_solution(12216923490258789091)
XLA Ops:
  0.0 0.8 %convert_element_type.63 = f32[256]{0:T(256)S(1)} convert(s32[256]{0:T(256)} %param.11) | non-fusion elementwise | flops 256 | bytes 2048 | tf_op jit(solution)/shard_map/convert_element_type | solution.py:55
  1.0 1.6 %convert_reduce_fusion = f32[16,256]{1,0:T(8,128)S(1)} fusion(bf16[16,256,128]{2,1,0:T(8,128)(2,1)} %param.10), kind=kLoop, calls=%fused_computation.1 | loop fusion | flops 1044480 | bytes 1064960 | tf_op jit(solution)/shard_map/reduce_sum | solution.py:16
  2.6 2.3 %fusion.2 = f32[16,256]{1,0:T(8,128)S(1)} fusion(bf16[16,256,128]{2,1,0:T(8,128)(2,1)} %param.10, f32[16,256]{1,0:T(8,128)S(1)} %broadcast_multiply_fusion.1), kind=kLoop, calls=%fused_computation.4 | loop fusion | flops 2093056 | bytes 1081344 | tf_op jit(solution)/shard_map/reduce_sum | solution.py:18
  4.9 1.3 %fusion.4 = bf16[16,256,128]{2,1,0:T(8,128)(2,1)S(1)} fusion(bf16[16,256,128]{2,1,0:T(8,128)(2,1)S(1)} %copy-done.1, f32[128]{0:T(128)S(1)} %copy-done.8, f32[16,256]{1,0:T(8,128)S(1)} %add_rsqrt_fusion, f32[16,256]{1,0:T(8,128)S(1)} %broadcast_multiply_fusion.1), kind=kLoop, calls=%fused_computation.6 | loop fusion | flops 2621440 | bytes 2130432 | tf_op jit(solution)/shard_map/convert_element_type | solution.py:58
  6.2 1.2 %fusion.31 = f32[16,256,512]{2,1,0:T(8,128)S(1)} fusion(bf16[16,256,128]{2,1,0:T(8,128)(2,1)S(1)} %fusion.4, bf16[128,128]{1,0:T(8,128)(2,1)S(1)} %copy-done.4, bf16[128,128]{1,0:T(8,128)(2,1)S(1)} %copy-done.5, bf16[128,128]{1,0:T(8,128)(2,1)S(1)} %copy-done.6, bf16[128,128]{1,0:T(8,128)(2,1)S(1)} %copy-done.7), kind=kOutput, calls=%fused_computation.41 | convolution fusion | flops 537395200 | bytes 9568256 | tf_op jit(solution)/shard_map/dot_general | solution.py:60
  7.5 2.0 %fusion.30 = (bf16[128,16,256]{0,2,1:T(8,128)(2,1)S(1)}, bf16[128,16,256]{0,2,1:T(8,128)(2,1)}) fusion(f32[16,256]{1,0:T(8,128)S(1)} %broadcast_multiply_fusion, f32[16,256,512]{2,1,0:T(8,128)S(1)} %fusion.31), kind=kLoop, calls=%fused_computation.39 | loop fusion | flops 6291456 | bytes 10502144 | tf_op jit(solution)/shard_map/transpose | solution.py:75
  9.5 1.8 %collective-permute-start = (bf16[128,16,256]{0,2,1:T(8,128)(2,1)S(1)}, bf16[128,16,256]{0,2,1:T(8,128)(2,1)}, u32[]{:S(2)}, u32[]{:S(2)}) collective-permute-start(bf16[128,16,256]{0,2,1:T(8,128)(2,1)S(1)} %get-tuple-element.5), channel_id=1, source_target_pairs={{15,0},{0,1},{1,2},{2,3},{3,4},{4,5},{5,6},{6,7},{7,8},{8,9},{9,10... | collective-permute-start | bytes 3145736 | tf_op jit(solution)/shard_map/ppermute | solution.py:12
  11.3 1.6 %copy.39 = bf16[16,256,128]{2,0,1:T(8,128)(2,1)} copy(bf16[16,256,128]{2,1,0:T(8,128)(2,1)S(1)} %copy-done.1) | data formatting | bytes 2097152 | tf_op args[0]
  13.0 5.0 %all-to-all-start = ((bf16[16,256,128]{2,0,1:T(8,128)(2,1)}), bf16[16,256,128]{2,0,1:T(8,128)(2,1)}, u32[]{:S(2)}, u32[]{:S(2)}) async-start(bf16[16,256,128]{2,0,1:T(8,128)(2,1)} %copy.39), calls=%async_computation | async-start | bytes 2097152 | tf_op jit(solution)/shard_map/all_to_all | solution.py:54
  18.0 1.7 %copy.42 = bf16[128,16,256]{2,1,0:T(8,128)(2,1)} copy(bf16[128,16,256]{0,2,1:T(8,128)(2,1)S(1)} %get-tuple-element.5) | data formatting | bytes 2097152 | tf_op jit(solution)/shard_map/transpose | solution.py:75
  19.7 1.9 %copy.41 = bf16[128,16,256]{2,1,0:T(8,128)(2,1)S(1)} copy(bf16[128,16,256]{0,2,1:T(8,128)(2,1)} %get-tuple-element.6) | data formatting | bytes 2097152 | tf_op jit(solution)/shard_map/transpose | solution.py:74
  21.6 2.6 %fusion.42 = f32[128,16,16]{2,1,0:T(8,128)} fusion(bf16[128,16,256]{2,1,0:T(8,128)(2,1)S(1)} %copy.41, bf16[128,16,256]{2,1,0:T(8,128)(2,1)} %copy.42), kind=kOutput, calls=%fused_computation.79 | convolution fusion | flops 16777216 | bytes 2228224 | tf_op jit(solution)/shard_map/cik,cjk->cij/dot_general | solution.py:26
  24.2 1.6 %copy.43 = f32[128,16,16]{0,2,1:T(8,128)S(1)} copy(f32[128,16,16]{2,1,0:T(8,128)} %fusion.42) | data formatting | bytes 262144 | tf_op jit(solution)/shard_map/cik,cjk->cij/dot_general | solution.py:26
  25.9 0.2 multiply_reduce_fusion.2
  26.1 9.0 %collective-permute-done = bf16[128,16,256]{0,2,1:T(8,128)(2,1)} collective-permute-done((bf16[128,16,256]{0,2,1:T(8,128)(2,1)S(1)}, bf16[128,16,256]{0,2,1:T(8,128)(2,1)}, u32[]{:S(2)}, u32[]{:S(2)}) %collective-permute-start) | collective-permute-done | bytes 1048608 | tf_op jit(solution)/shard_map/ppermute | solution.py:12
  35.1 3.6 %collective-permute-start.2 = (bf16[128,16,256]{0,2,1:T(8,128)(2,1)}, bf16[128,16,256]{0,2,1:T(8,128)(2,1)}, u32[]{:S(2)}, u32[]{:S(2)}) collective-permute-start(bf16[128,16,256]{0,2,1:T(8,128)(2,1)} %collective-permute-done), channel_id=1, source_target_pairs={{15,0},{0,1},{1,2},{2,3},{3,4},{4,5},{5,6},{6,7},{7,8},{8,9},{9,10... | collective-permute-start | bytes 3145736 | tf_op jit(solution)/shard_map/ppermute | solution.py:12
  38.7 0.7 constant_dynamic-slice_fusion.1
  39.4 1.9 %copy.45 = bf16[128,16,256]{2,1,0:T(8,128)(2,1)S(1)} copy(bf16[128,16,256]{0,2,1:T(8,128)(2,1)} %collective-permute-done) | data formatting | bytes 2097152 | tf_op jit(solution)/shard_map/ppermute | solution.py:12
  41.3 0.4 fusion.44
  41.7 0.4 copy.46
  42.2 0.2 multiply_reduce_fusion.1
  42.4 16.2 %all-to-all-done = bf16[16,256,128]{2,0,1:T(8,128)(2,1)} async-done(((bf16[16,256,128]{2,0,1:T(8,128)(2,1)}), bf16[16,256,128]{2,0,1:T(8,128)(2,1)}, u32[]{:S(2)}, u32[]{:S(2)}) %all-to-all-start) | async-done | bytes 1048608 | tf_op jit(solution)/shard_map/all_to_all | solution.py:54
  58.6 2.5 %copy.40 = bf16[16,16,16,128]{3,2,1,0:T(8,128)(2,1)} copy(bf16[16,16,16,128]{3,1,2,0:T(8,128)(2,1)} %bitcast.1) | data formatting | bytes 2097152 | tf_op jit(solution)/shard_map/all_to_all | solution.py:54
  61.1 1.9 %copy.48 = bf16[128,16,256]{2,1,0:T(8,128)(2,1)S(1)} copy(bf16[128,16,256]{0,2,1:T(8,128)(2,1)} %collective-permute-done.2) | data formatting | bytes 2097152 | tf_op jit(solution)/shard_map/ppermute | solution.py:12
  62.9 0.4 fusion.46
  63.4 0.4 copy.49
  64.1 0.3 multiply_convert_fusion
  64.8 0.4 collective-permute-start.1
  66.0 1.5 %fusion.38 = bf16[256,16,128]{2,1,0:T(8,128)(2,1)} fusion(bf16[256,16,128]{2,1,0:T(8,128)(2,1)} %bitcast.60, s32[]{:T(128)S(6)} %select_n.48, f32[16,16,128]{2,1,0:T(8,128)S(1)} %bitcast.64), kind=kLoop, calls=%fused_computation.63 | loop fusion | flops 98304 | bytes 262148 | tf_op jit(solution)/shard_map/dynamic_update_slice | solution.py:106
  67.5 2.4 %collective-permute-done.1 = bf16[16,16,128]{2,1,0:T(8,128)(2,1)S(1)} collective-permute-done((bf16[16,16,128]{2,1,0:T(8,128)(2,1)S(1)}, bf16[16,16,128]{2,1,0:T(8,128)(2,1)S(1)}, u32[]{:S(2)}, u32[]{:S(2)}) %collective-permute-start.1) | collective-permute-done | bytes 65568 | tf_op jit(solution)/shard_map/ppermute | solution.py:12
  69.8 1.5 %fusion.39 = bf16[256,16,128]{2,1,0:T(8,128)(2,1)} fusion(bf16[256,16,128]{2,1,0:T(8,128)(2,1)} %fusion.38, s32[]{:T(128)S(6)} %select_n.51, bf16[16,16,128]{2,1,0:T(8,128)(2,1)S(1)} %collective-permute-done.1), kind=kLoop, calls=%fused_computation.64 | loop fusion | flops 131072 | bytes 196612 | tf_op jit(solution)/shard_map/dynamic_update_slice | solution.py:106
  71.3 1.5 %fusion.40 = bf16[256,16,128]{2,1,0:T(8,128)(2,1)} fusion(bf16[256,16,128]{2,1,0:T(8,128)(2,1)} %fusion.39, s32[]{:T(128)S(6)} %select_n.55, bf16[16,16,128]{2,1,0:T(8,128)(2,1)S(1)} %collective-permute-done.3), kind=kLoop, calls=%fused_computation.65 | loop fusion | flops 131072 | bytes 196612 | tf_op jit(solution)/shard_map/dynamic_update_slice | solution.py:106
  (44 shorter events, 1.7 us)
Async XLA Ops:
  0.0 64.4 %copy-start = (bf16[128,128]{1,0:T(8,128)(2,1)S(1)}, bf16[128,128]{1,0:T(8,128)(2,1)}, u32[]{:S(2)}) copy-start(bf16[128,128]{1,0:T(8,128)(2,1)} %param.19) | copy-start | bytes 98308
  0.0 4.9 %copy-start.1 = (bf16[16,256,128]{2,1,0:T(8,128)(2,1)S(1)}, bf16[16,256,128]{2,1,0:T(8,128)(2,1)}, u32[]{:S(2)}) copy-start(bf16[16,256,128]{2,1,0:T(8,128)(2,1)} %param.10) | copy-start | bytes 3145732
  0.0 4.9 %copy-start.8 = (f32[128]{0:T(128)S(1)}, f32[128]{0:T(128)}, u32[]{:S(2)}) copy-start(f32[128]{0:T(128)} %param.12) | copy-start | bytes 1540
  0.9 5.3 %copy-start.4 = (bf16[128,128]{1,0:T(8,128)(2,1)S(1)}, bf16[128,128]{1,0:T(8,128)(2,1)}, u32[]{:S(2)}) copy-start(bf16[128,128]{1,0:T(8,128)(2,1)} %param.16) | copy-start | bytes 98308
  0.9 5.3 %copy-start.5 = (bf16[128,128]{1,0:T(8,128)(2,1)S(1)}, bf16[128,128]{1,0:T(8,128)(2,1)}, u32[]{:S(2)}) copy-start(bf16[128,128]{1,0:T(8,128)(2,1)} %param.15) | copy-start | bytes 98308
  0.9 5.3 %copy-start.6 = (bf16[128,128]{1,0:T(8,128)(2,1)S(1)}, bf16[128,128]{1,0:T(8,128)(2,1)}, u32[]{:S(2)}) copy-start(bf16[128,128]{1,0:T(8,128)(2,1)} %param.14) | copy-start | bytes 98308
  0.9 5.3 %copy-start.7 = (bf16[128,128]{1,0:T(8,128)(2,1)S(1)}, bf16[128,128]{1,0:T(8,128)(2,1)}, u32[]{:S(2)}) copy-start(bf16[128,128]{1,0:T(8,128)(2,1)} %param.13) | copy-start | bytes 98308
  9.5 25.6 %collective-permute-start = (bf16[128,16,256]{0,2,1:T(8,128)(2,1)S(1)}, bf16[128,16,256]{0,2,1:T(8,128)(2,1)}, u32[]{:S(2)}, u32[]{:S(2)}) collective-permute-start(bf16[128,16,256]{0,2,1:T(8,128)(2,1)S(1)} %get-tuple-element.5), channel_id=1, source_target_pairs={{15,0},{0,1},{1,2},{2,3},{3,4},{4,5},{5,6},{6,7},{7,8},{8,9},{9,10... | collective-permute-start | bytes 3145736 | tf_op jit(solution)/shard_map/ppermute | solution.py:12
  13.0 45.6 %all-to-all-start = ((bf16[16,256,128]{2,0,1:T(8,128)(2,1)}), bf16[16,256,128]{2,0,1:T(8,128)(2,1)}, u32[]{:S(2)}, u32[]{:S(2)}) async-start(bf16[16,256,128]{2,0,1:T(8,128)(2,1)} %copy.39), calls=%async_computation | async-start | bytes 2097152 | tf_op jit(solution)/shard_map/all_to_all | solution.py:54
  35.1 26.0 %collective-permute-start.2 = (bf16[128,16,256]{0,2,1:T(8,128)(2,1)}, bf16[128,16,256]{0,2,1:T(8,128)(2,1)}, u32[]{:S(2)}, u32[]{:S(2)}) collective-permute-start(bf16[128,16,256]{0,2,1:T(8,128)(2,1)} %collective-permute-done), channel_id=1, source_target_pairs={{15,0},{0,1},{1,2},{2,3},{3,4},{4,5},{5,6},{6,7},{7,8},{8,9},{9,10... | collective-permute-start | bytes 3145736 | tf_op jit(solution)/shard_map/ppermute | solution.py:12
  62.9 1.2 %copy-start.9 = (f32[128]{0:T(128)S(1)}, f32[128]{0:T(128)}, u32[]{:S(2)}) copy-start(f32[128]{0:T(128)} %param.18) | copy-start | bytes 1540
  63.3 1.2 %copy-start.3 = (bf16[16,16,128]{2,1,0:T(8,128)(2,1)S(1)}, bf16[16,16,128]{2,1,0:T(8,128)(2,1)}, u32[]{:S(2)}) copy-start(bf16[16,16,128]{2,1,0:T(8,128)(2,1)} %get-tuple-element.8) | copy-start | bytes 196612
  63.4 1.2 %copy-start.10 = (bf16[128,128]{1,0:T(8,128)(2,1)S(1)}, bf16[128,128]{1,0:T(8,128)(2,1)}, u32[]{:S(2)}) copy-start(bf16[128,128]{1,0:T(8,128)(2,1)} %param.17) | copy-start | bytes 98308
  63.4 2.2 %copy-start.2 = (bf16[16,16,128]{2,1,0:T(8,128)(2,1)S(1)}, bf16[16,16,128]{2,1,0:T(8,128)(2,1)}, u32[]{:S(2)}) copy-start(bf16[16,16,128]{2,1,0:T(8,128)(2,1)} %get-tuple-element.7) | copy-start | bytes 196612
  64.8 5.1 %collective-permute-start.1 = (bf16[16,16,128]{2,1,0:T(8,128)(2,1)S(1)}, bf16[16,16,128]{2,1,0:T(8,128)(2,1)S(1)}, u32[]{:S(2)}, u32[]{:S(2)}) collective-permute-start(bf16[16,16,128]{2,1,0:T(8,128)(2,1)S(1)} %bitcast.68), channel_id=1, source_target_pairs={{1,0},{2,1},{3,2},{4,3},{5,4},{6,5},{7,6},{8,7},{9,8},{10,9},{11,1... | collective-permute-start | bytes 196616 | tf_op jit(solution)/shard_map/ppermute | solution.py:12
  65.7 5.6 %collective-permute-start.3 = (bf16[16,16,128]{2,1,0:T(8,128)(2,1)S(1)}, bf16[16,16,128]{2,1,0:T(8,128)(2,1)S(1)}, u32[]{:S(2)}, u32[]{:S(2)}) collective-permute-start(bf16[16,16,128]{2,1,0:T(8,128)(2,1)S(1)} %bitcast.69), channel_id=1, source_target_pairs={{2,0},{3,1},{4,2},{5,3},{6,4},{7,5},{8,6},{9,7},{10,8},{11,9},{12,... | collective-permute-start | bytes 196616 | tf_op jit(solution)/shard_map/ppermute | solution.py:12
where the time goes:
time: 73.4 us; the launch traced here: 72.8 us
  waiting for transfers between devices  27.6 us (38%)
  local copies, waits for them, and re-layouts  14.6 us (20%)
  other arithmetic  13.7 us (19%)
  starting transfers between devices  11 us (15%)
  matrix products  5.59 us (8%)
    all_to_all x1, waiting for transfers between devices, shards(): lax.all_to_all(pair, 'row', split_axis=1, concat_axis=0, tiled=True)  16.2 us
    ppermute x4, waiting for transfers between devices, passed_along(): return lax.ppermute(block, axis, route)  11.4 us
    ppermute x4, starting transfers between devices, passed_along(): return lax.ppermute(block, axis, route)  5.93 us
    all_to_all x1, starting transfers between devices, shards(): lax.all_to_all(pair, 'row', split_axis=1, concat_axis=0, tiled=True)  5.04 us
    dynamic_update_slice x3, other arithmetic, shards(): lax.dynamic_update_slice_in_dim(columns_now, new_block, start, 0)  4.47 us
    ppermute x2, local copies, waits for them, and re-layouts, passed_along(): return lax.ppermute(block, axis, route)  3.72 us
    dot_general x3, matrix products, band_update(): jnp.einsum('cik,cjk->cij', left_cols, right_cols, preferred_element_type=...  3.41 us
    reduce_sum x4, other arithmetic, normalize(): spread = jnp.mean(centered * centered, axis=-1, keepdims=True)  2.9 us
  transfers between devices with their start and end apart: 5, of which 3 were waited for; matrix products, arithmetic and copies ran while one was open for 27% of the time, Pallas kernels for 0%

commit v1 on v0

v1 whole, which is shorter than its diff:
```python
import functools

import jax
import jax.numpy as jnp
from jax import lax
from jax.experimental import pallas as pl
from jax.experimental.pallas import tpu as pltpu
from jax.sharding import PartitionSpec as P

EPSILON = 1e-05
MESH = pl.DeviceIdType.MESH
CHUNKS = 4
STEPS = 4


def normalize(values, gain):
    center = jnp.mean(values, axis=-1, keepdims=True)
    centered = values - center
    spread = jnp.mean(centered * centered, axis=-1, keepdims=True)
    return centered * lax.rsqrt(spread + EPSILON) * gain


def dot(a, b):
    return jnp.dot(a, b, preferred_element_type=jnp.float32)


def kernel(
    blocks,
    pair,
    mask,
    in_gain,
    w_a_gate,
    w_a_proj,
    w_b_gate,
    w_b_proj,
    w_out_gate,
    out_gain,
    w_out,
    out,
    halo,
    left,
    right,
    product,
    token_mask,
    halo_send,
    halo_recv,
    forward_send,
    block_send,
    block_recv,
):
    rows, tokens, channels = pair.shape
    me = lax.axis_index("row")
    odd = lax.rem(me, 2)
    part = rows // CHUNKS
    own = pl.multiple_of(me * rows, rows)

    def at(distance):
        return {"row": lax.rem(me + distance + blocks, blocks)}

    barrier = pltpu.get_barrier_semaphore()

    def greet(distance, _):
        pl.semaphore_signal(barrier, inc=1, device_id=at(distance), device_id_type=MESH)
        return 0

    lax.fori_loop(1, blocks, greet, 0)
    pl.semaphore_wait(barrier, blocks - 1)

    def halo_copy(distance, chunk):
        slot = distance - 1
        piece = pl.ds(chunk * part, part)
        return pltpu.make_async_remote_copy(
            src_ref=pair.at[piece],
            dst_ref=halo.at[slot, piece],
            send_sem=halo_send.at[slot, chunk],
            recv_sem=halo_recv.at[slot, chunk],
            device_id=at(-distance),
            device_id_type=MESH,
        )

    half = CHUNKS // 2

    def halo_all(act):
        for chunk in range(half):
            act(halo_copy(2, chunk))
            pl.when(odd == 0)(lambda chunk=chunk: act(halo_copy(1, half + chunk)))
            pl.when(odd == 1)(lambda chunk=chunk: act(halo_copy(2, half + chunk)))
        for chunk in range(half):
            pl.when(odd == 1)(lambda chunk=chunk: act(halo_copy(1, chunk)))
            pl.when(odd == 1)(lambda chunk=chunk: act(halo_copy(1, half + chunk)))

    halo_all(lambda copy: copy.start())

    def block_copy(distance):
        target = lax.rem(me + distance, blocks)
        columns = pl.ds(pl.multiple_of(target * rows, rows), rows)
        return pltpu.make_async_remote_copy(
            src_ref=pair.at[:, columns],
            dst_ref=out.at[pl.ds(own, rows)],
            send_sem=block_send.at[distance],
            recv_sem=block_recv.at[distance],
            device_id={"row": target},
            device_id_type=MESH,
        )

    def send_block(distance, _):
        block_copy(distance).start()
        return 0

    lax.fori_loop(1, blocks - 2, send_block, 0)

    mask_row = mask[...].astype(jnp.float32)
    token_mask[...] = jnp.broadcast_to(mask_row, (channels, tokens)).T

    def make_right(i, _):
        normed = normalize(pair[i].astype(jnp.float32), in_gain[...]).astype(jnp.bfloat16)
        values = jax.nn.sigmoid(dot(normed, w_b_gate[...])) * dot(normed, w_b_proj[...])
        values = values * token_mask[...] * token_mask[pl.ds(own + i, 1), :]
        right[i] = values.astype(jnp.bfloat16).astype(jnp.float32)
        return 0

    lax.fori_loop(0, rows, make_right, 0)

    def process(read, owner):
        def make_left(i, _):
            normed = normalize(read(i).astype(jnp.float32), in_gain[...]).astype(jnp.bfloat16)
            values = jax.nn.sigmoid(dot(normed, w_a_gate[...])) * dot(normed, w_a_proj[...])
            left[i] = values.astype(jnp.bfloat16).astype(jnp.float32)
            return 0

        lax.fori_loop(0, rows, make_left, 0)
        first = pl.multiple_of(owner * rows, rows)

        def tile(t, _):
            i = (t // (rows // 8)) * 2
            j = pl.multiple_of((t % (rows // 8)) * 8, 8)

            def body(step, sums):
                sums = list(sums)
                for s in range(STEPS):
                    k = pl.ds(pl.multiple_of(step * (8 * STEPS) + s * 8, 8), 8)
                    ls = [left[i + a, k, :] for a in range(2)]
                    for b in range(8):
                        r = right[j + b, k, :]
                        for a in range(2):
                            sums[a * 8 + b] = sums[a * 8 + b] + ls[a] * r
                return tuple(sums)

            zero = jnp.zeros((8, channels), jnp.float32)
            sums = lax.fori_loop(0, tokens // (8 * STEPS), body, (zero,) * 16)
            for a in range(2):
                joined = jnp.concatenate(
                    [jnp.sum(sums[a * 8 + b], axis=0, keepdims=True) for b in range(8)], axis=0
                )
                product[i + a, pl.ds(j, 8), :] = joined * token_mask[pl.ds(first + i + a, 1), :]
            return 0

        lax.fori_loop(0, (rows // 2) * (rows // 8), tile, 0)
        normed_x = normalize(product[...], out_gain[...]).astype(jnp.bfloat16)
        update = dot(normed_x.reshape(rows * rows, channels), w_out[...])
        old = read(slice(None), pl.ds(own, rows)).astype(jnp.float32)
        normed = normalize(old, in_gain[...]).astype(jnp.bfloat16)
        gating = jax.nn.sigmoid(dot(normed.reshape(rows * rows, channels), w_out_gate[...]))
        new = old + (gating * update).reshape(rows, rows, channels)
        out[pl.ds(first, rows)] = new.astype(jnp.bfloat16)

    process(lambda *index: pair[index], me)

    def arrival(slot, chunk):
        piece = pl.ds(chunk * part, part)
        return pltpu.make_async_remote_copy(
            src_ref=pair.at[piece],
            dst_ref=halo.at[slot, piece],
            send_sem=halo_send.at[slot, chunk],
            recv_sem=halo_recv.at[slot, chunk],
            device_id=at(1 - 2 * odd),
            device_id_type=MESH,
        )

    def forward(c):
        chunk = odd * half + c
        piece = pl.ds(chunk * part, part)
        return pltpu.make_async_remote_copy(
            src_ref=halo.at[1 - odd, piece],
            dst_ref=halo.at[odd, piece],
            send_sem=forward_send.at[c],
            recv_sem=halo_recv.at[odd, chunk],
            device_id=at(1 - 2 * odd),
            device_id_type=MESH,
        )

    for c in range(half):
        arrival(1 - odd, odd * half + c).wait_recv()
        forward(c).start()

    def halo_step(step, _):
        slot = lax.rem(odd + step, 2)

        @pl.when(step == 0)
        def _():
            for chunk in range(CHUNKS):
                arrival(odd, chunk).wait_recv()

        @pl.when(step == 1)
        def _():
            for c in range(half):
                arrival(1 - odd, (1 - odd) * half + c).wait_recv()

        process(lambda *index: halo[(slot,) + index], lax.rem(me + 1 + slot, blocks))
        return 0

    lax.fori_loop(0, 2, halo_step, 0)

    for c in range(half):
        forward(c).wait_send()
    halo_all(lambda copy: copy.wait_send())

    def finish_block(distance, _):
        source = lax.rem(me - distance + blocks, blocks)
        columns = pl.ds(own, rows)
        landed = pltpu.make_async_remote_copy(
            src_ref=pair.at[:, columns],
            dst_ref=out.at[pl.ds(pl.multiple_of(source * rows, rows), rows)],
            send_sem=block_send.at[distance],
            recv_sem=block_recv.at[distance],
            device_id={"row": source},
            device_id_type=MESH,
        )
        landed.wait_recv()
        block_copy(distance).wait_send()
        return 0

    lax.fori_loop(1, blocks - 2, finish_block, 0)


def shards(blocks, pair, residue_mask, ln_in_gain, *rest):
    w_a_gate, w_a_proj, w_b_gate, w_b_proj, w_out_gate, ln_out_gain, w_out = rest
    rows, tokens, channels = pair.shape
    vmem = pl.BlockSpec(memory_space=pltpu.VMEM)
    return pl.pallas_call(
        functools.partial(kernel, blocks),
        out_shape=jax.ShapeDtypeStruct((tokens, rows, channels), jnp.bfloat16),
        in_specs=[vmem] * 10,
        out_specs=vmem,
        scratch_shapes=[
            pltpu.VMEM((2, rows, tokens, channels), jnp.bfloat16),
            pltpu.VMEM((rows, tokens, channels), jnp.float32),
            pltpu.VMEM((rows, tokens, channels), jnp.float32),
            pltpu.VMEM((rows, rows, channels), jnp.float32),
            pltpu.VMEM((tokens, channels), jnp.float32),
            pltpu.SemaphoreType.DMA((2, CHUNKS)),
            pltpu.SemaphoreType.DMA((2, CHUNKS)),
            pltpu.SemaphoreType.DMA((CHUNKS // 2,)),
            pltpu.SemaphoreType.DMA((blocks,)),
            pltpu.SemaphoreType.DMA((blocks,)),
        ],
        compiler_params=pltpu.CompilerParams(
            collective_id=0, has_side_effects=True, vmem_limit_bytes=48 * 2**20
        ),
    )(
        pair,
        residue_mask.reshape(1, tokens),
        ln_in_gain.reshape(1, channels),
        w_a_gate,
        w_a_proj,
        w_b_gate,
        w_b_proj,
        w_out_gate,
        ln_out_gain.reshape(1, channels),
        w_out,
    )


def solution(mesh):
    placed = (P(("groups", "row"), None, None), P("groups"), P(), P(), P(), P(), P(), P(), P(), P())
    return jax.shard_map(
        functools.partial(shards, mesh.shape["row"]),
        mesh=mesh,
        in_specs=placed,
        out_specs=P("groups", "row", None),
        check_vma=False,
    )
```

time: 73.4 us -> 66.4 us (0.905)
  Pallas kernels: 0 us -> 58.4 us
  waiting for transfers between devices: 27.6 us -> 0 us
  other arithmetic: 13.7 us -> 0 us
  starting transfers between devices: 11 us -> 0 us
  local copies, waits for them, and re-layouts: 14.6 us -> 7.43 us
  matrix products: 5.59 us -> 0 us
    pallas_call x0 -> x1, Pallas kernels: none -> 58.4 us  [shards(): pl.pallas_call(functools.partial(kernel, blocks), out_shape=jax.ShapeDtyp...]
    all_to_all x1 -> x0, waiting for transfers between devices: 16.2 us -> none  [shards(): lax.all_to_all(pair, 'row', split_axis=1, concat_axis=0, tiled=True)]
    ppermute x4 -> x0, waiting for transfers between devices: 11.4 us -> none  [passed_along(): return lax.ppermute(block, axis, route)]
    ppermute x4 -> x0, starting transfers between devices: 5.93 us -> none  [passed_along(): return lax.ppermute(block, axis, route)]
    unnamed x23 -> x21, local copies, waits for them, and re-layouts: 1.7 us -> 7.43 us
    dot_general x10 -> x0, matrix products: 5.59 us -> none  [the longest x3 3.41 us: band_update(): jnp.einsum('cik,cjk->cij', left_cols, right_cols, preferred_element_type=...]
    all_to_all x1 -> x0, starting transfers between devices: 5.04 us -> none  [shards(): lax.all_to_all(pair, 'row', split_axis=1, concat_axis=0, tiled=True)]
    reduce_sum x8 -> x0, other arithmetic: 4.81 us -> none  [the longest x4 2.9 us: normalize(): spread = jnp.mean(centered * centered, axis=-1, keepdims=True)]
  transfers between devices with their start and end apart: 5 -> 0, of which waited for: 3 -> 0; matrix products, arithmetic and copies ran while one was open for 27% -> 0% of each run, Pallas kernels for 0% -> 0%
where the time goes in v1:
time: 66.4 us; the launch traced here: 65.9 us
  Pallas kernels  58.4 us (88%)
  local copies, waits for them, and re-layouts  7.43 us (11%)
    pallas_call x1, Pallas kernels, shards(): pl.pallas_call(functools.partial(kernel, blocks), out_shape=jax.ShapeDtyp...  58.4 us
    unnamed x21, local copies, waits for them, and re-layouts  7.43 us

profile of v1, /device:TPU:15, one launch (start us, length us, event | category | flops | bytes accessed | tf_op | source)
XLA Modules:
  0.0 65.9 jit_solution(4994109771449881444)
XLA Ops:
  0.0 0.0 copy-start.9
  0.0 0.0 copy-start.7
  0.0 0.0 copy-start.8
  0.0 0.6 copy-done.9
  0.7 0.0 copy-done.7
  0.7 0.0 copy-done.8
  0.7 0.0 copy-start
  0.7 1.2 %copy-done = bf16[16,256,128]{2,1,0:T(8,128)(2,1)S(1)} copy-done((bf16[16,256,128]{2,1,0:T(8,128)(2,1)S(1)}, bf16[16,256,128]{2,1,0:T(8,128)(2,1)}, u32[]{:S(2)}) %copy-start) | copy-done | bytes 1048600
  1.9 0.0 copy-start.1
  1.9 0.8 %copy-done.1 = bf16[128,128]{1,0:T(8,128)(2,1)S(1)} copy-done((bf16[128,128]{1,0:T(8,128)(2,1)S(1)}, bf16[128,128]{1,0:T(8,128)(2,1)}, u32[]{:S(2)}) %copy-start.1) | copy-done | bytes 32792
  2.7 0.0 copy-start.2
  2.7 0.8 %copy-done.2 = bf16[128,128]{1,0:T(8,128)(2,1)S(1)} copy-done((bf16[128,128]{1,0:T(8,128)(2,1)S(1)}, bf16[128,128]{1,0:T(8,128)(2,1)}, u32[]{:S(2)}) %copy-start.2) | copy-done | bytes 32792
  3.4 0.0 copy-start.3
  3.4 0.8 %copy-done.3 = bf16[128,128]{1,0:T(8,128)(2,1)S(1)} copy-done((bf16[128,128]{1,0:T(8,128)(2,1)S(1)}, bf16[128,128]{1,0:T(8,128)(2,1)}, u32[]{:S(2)}) %copy-start.3) | copy-done | bytes 32792
  4.2 0.0 copy-start.4
  4.2 0.8 %copy-done.4 = bf16[128,128]{1,0:T(8,128)(2,1)S(1)} copy-done((bf16[128,128]{1,0:T(8,128)(2,1)S(1)}, bf16[128,128]{1,0:T(8,128)(2,1)}, u32[]{:S(2)}) %copy-start.4) | copy-done | bytes 32792
  5.0 0.0 copy-start.5
  5.0 0.8 %copy-done.5 = bf16[128,128]{1,0:T(8,128)(2,1)S(1)} copy-done((bf16[128,128]{1,0:T(8,128)(2,1)S(1)}, bf16[128,128]{1,0:T(8,128)(2,1)}, u32[]{:S(2)}) %copy-start.5) | copy-done | bytes 32792
  5.7 0.0 copy-start.6
  5.7 0.8 %copy-done.6 = bf16[128,128]{1,0:T(8,128)(2,1)S(1)} copy-done((bf16[128,128]{1,0:T(8,128)(2,1)S(1)}, bf16[128,128]{1,0:T(8,128)(2,1)}, u32[]{:S(2)}) %copy-start.6) | copy-done | bytes 32792
  6.5 58.4 %shard_map.100 = bf16[256,16,128]{2,1,0:T(8,128)(2,1)S(1)} custom-call(bf16[16,256,128]{2,1,0:T(8,128)(2,1)S(1)} %copy-done, s32[1,256]{1,0:T(1,128)S(1)} %bitcast.3, f32[1,128]{1,0:T(1,128)S(1)} %bitcast.4, bf16[128,128]{1,0:T(8,128)(2,1)S(1)} %copy-done.1, bf16[128,128]{1,0:T(8,128)(2,1)S(1)} %copy-done.2, bf16[128,128]{1,0:T(8,128)(2,1)S(1)} %copy-done.3, ...), custom_call_target="tpu_custom_call" | custom-call | tf_op jit(solution)/shard_map/pallas_call | solution.py:240
  64.9 1.0 %copy.12 = bf16[256,16,128]{2,1,0:T(8,128)(2,1)} copy(bf16[256,16,128]{2,1,0:T(8,128)(2,1)S(1)} %shard_map.100) | data formatting | bytes 2097152
Async XLA Ops:
  0.0 0.7 copy-start.9
  0.0 0.7 %copy-start.7 = (s32[256]{0:T(256)S(1)}, s32[256]{0:T(256)}, u32[]{:S(2)}) copy-start(s32[256]{0:T(256)} %param.11) | copy-start | bytes 3076
  0.0 0.7 %copy-start.8 = (f32[128]{0:T(128)S(1)}, f32[128]{0:T(128)}, u32[]{:S(2)}) copy-start(f32[128]{0:T(128)} %param.12) | copy-start | bytes 1540
  0.7 1.2 %copy-start = (bf16[16,256,128]{2,1,0:T(8,128)(2,1)S(1)}, bf16[16,256,128]{2,1,0:T(8,128)(2,1)}, u32[]{:S(2)}) copy-start(bf16[16,256,128]{2,1,0:T(8,128)(2,1)} %pair.1) | copy-start | bytes 3145732
  1.9 0.8 %copy-start.1 = (bf16[128,128]{1,0:T(8,128)(2,1)S(1)}, bf16[128,128]{1,0:T(8,128)(2,1)}, u32[]{:S(2)}) copy-start(bf16[128,128]{1,0:T(8,128)(2,1)} %w_a_gate.1) | copy-start | bytes 98308
  2.7 0.8 %copy-start.2 = (bf16[128,128]{1,0:T(8,128)(2,1)S(1)}, bf16[128,128]{1,0:T(8,128)(2,1)}, u32[]{:S(2)}) copy-start(bf16[128,128]{1,0:T(8,128)(2,1)} %w_a_proj.1) | copy-start | bytes 98308
  3.4 0.8 %copy-start.3 = (bf16[128,128]{1,0:T(8,128)(2,1)S(1)}, bf16[128,128]{1,0:T(8,128)(2,1)}, u32[]{:S(2)}) copy-start(bf16[128,128]{1,0:T(8,128)(2,1)} %w_b_gate.1) | copy-start | bytes 98308
  4.2 0.8 %copy-start.4 = (bf16[128,128]{1,0:T(8,128)(2,1)S(1)}, bf16[128,128]{1,0:T(8,128)(2,1)}, u32[]{:S(2)}) copy-start(bf16[128,128]{1,0:T(8,128)(2,1)} %w_b_proj.1) | copy-start | bytes 98308
  5.0 0.8 %copy-start.5 = (bf16[128,128]{1,0:T(8,128)(2,1)S(1)}, bf16[128,128]{1,0:T(8,128)(2,1)}, u32[]{:S(2)}) copy-start(bf16[128,128]{1,0:T(8,128)(2,1)} %w_out_gate.1) | copy-start | bytes 98308
  5.7 0.8 %copy-start.6 = (bf16[128,128]{1,0:T(8,128)(2,1)S(1)}, bf16[128,128]{1,0:T(8,128)(2,1)}, u32[]{:S(2)}) copy-start(bf16[128,128]{1,0:T(8,128)(2,1)} %w_out.1) | copy-start | bytes 98308

commit v2 on v1

--- a/solution.py
+++ b/solution.py
@@ -11,6 +11,8 @@
 MESH = pl.DeviceIdType.MESH
 CHUNKS = 4
 STEPS = 4
+GROUP = 1024
+LIMIT = 63 * 2**20
 
 
 def normalize(values, gain):
@@ -20,6 +22,10 @@
     return centered * lax.rsqrt(spread + EPSILON) * gain
 
 
+def half_sigmoid(values):
+    return 1.0 + jnp.tanh(0.5 * values)
+
+
 def dot(a, b):
     return jnp.dot(a, b, preferred_element_type=jnp.float32)
 
@@ -27,16 +33,24 @@
 def kernel(
     blocks,
     pair,
-    mask,
-    in_gain,
+    mask_arg,
+    in_gain_arg,
     w_a_gate,
     w_a_proj,
     w_b_gate,
     w_b_proj,
+    w_out_gate_arg,
+    out_gain_arg,
+    w_out_arg,
+    out,
+    own_pair,
+    mask,
+    in_gain,
+    w_in,
     w_out_gate,
     out_gain,
     w_out,
-    out,
+    load,
     halo,
     left,
     right,
@@ -64,30 +78,49 @@
         return 0
 
     lax.fori_loop(1, blocks, greet, 0)
+    loads = [(pair, own_pair), (mask_arg, mask), (in_gain_arg, in_gain)]
+    for n, w in enumerate((w_a_gate, w_a_proj, w_b_gate, w_b_proj)):
+        loads.append((w, w_in.at[:, n * channels : (n + 1) * channels]))
+    loads += [(w_out_gate_arg, w_out_gate), (out_gain_arg, out_gain), (w_out_arg, w_out)]
+    loads = [pltpu.make_async_copy(a, b, load.at[n]) for n, (a, b) in enumerate(loads)]
+    for copy in loads:
+        copy.start()
     pl.semaphore_wait(barrier, blocks - 1)
 
-    def halo_copy(distance, chunk):
-        slot = distance - 1
-        piece = pl.ds(chunk * part, part)
-        return pltpu.make_async_remote_copy(
-            src_ref=pair.at[piece],
-            dst_ref=halo.at[slot, piece],
-            send_sem=halo_send.at[slot, chunk],
-            recv_sem=halo_recv.at[slot, chunk],
+    half = CHUNKS // 2
+
+    def span(chunk):
+        return pl.ds(chunk * part, part)
+
+    def distance_of(chunk):
+        return 1 + odd if chunk >= half else 2
+
+    def direct(chunk):
+        distance = distance_of(chunk)
+        return pltpu.make_async_remote_copy(
+            src_ref=pair.at[span(chunk)],
+            dst_ref=halo.at[distance - 1, span(chunk)],
+            send_sem=halo_send.at[0, chunk],
+            recv_sem=halo_recv.at[distance - 1, chunk],
             device_id=at(-distance),
             device_id_type=MESH,
         )
 
-    half = CHUNKS // 2
+    def inner(chunk):
+        return pltpu.make_async_remote_copy(
+            src_ref=pair.at[span(chunk)],
+            dst_ref=halo.at[0, span(chunk)],
+            send_sem=halo_send.at[1, chunk],
+            recv_sem=halo_recv.at[0, chunk],
+            device_id=at(-1),
+            device_id_type=MESH,
+        )
 
     def halo_all(act):
-        for chunk in range(half):
-            act(halo_copy(2, chunk))
-            pl.when(odd == 0)(lambda chunk=chunk: act(halo_copy(1, half + chunk)))
-            pl.when(odd == 1)(lambda chunk=chunk: act(halo_copy(2, half + chunk)))
-        for chunk in range(half):
-            pl.when(odd == 1)(lambda chunk=chunk: act(halo_copy(1, chunk)))
-            pl.when(odd == 1)(lambda chunk=chunk: act(halo_copy(1, half + chunk)))
+        for chunk in range(CHUNKS):
+            act(direct(chunk))
+        for chunk in range(CHUNKS):
+            pl.when(odd == 1)(lambda chunk=chunk: act(inner(chunk)))
 
     halo_all(lambda copy: copy.start())
 
@@ -109,26 +142,43 @@
 
     lax.fori_loop(1, blocks - 2, send_block, 0)
 
-    mask_row = mask[...].astype(jnp.float32)
-    token_mask[...] = jnp.broadcast_to(mask_row, (channels, tokens)).T
-
-    def make_right(i, _):
-        normed = normalize(pair[i].astype(jnp.float32), in_gain[...]).astype(jnp.bfloat16)
-        values = jax.nn.sigmoid(dot(normed, w_b_gate[...])) * dot(normed, w_b_proj[...])
-        values = values * token_mask[...] * token_mask[pl.ds(own + i, 1), :]
-        right[i] = values.astype(jnp.bfloat16).astype(jnp.float32)
-        return 0
-
-    lax.fori_loop(0, rows, make_right, 0)
+    for copy in loads:
+        copy.wait()
+    token_mask[...] = jnp.broadcast_to(mask[...].astype(jnp.float32), (channels, tokens)).T
+
+    batch = max(1, GROUP // tokens)
+
+    def normed_of(values):
+        single = jnp.full((channels, channels), 1.0 / channels, jnp.bfloat16)
+        double = jnp.full((2 * channels, channels), 1.0 / channels, jnp.bfloat16)
+        centered = values.astype(jnp.float32) - dot(values, single)
+        square = centered * centered
+        high = square.astype(jnp.bfloat16)
+        low = (square - high.astype(jnp.float32)).astype(jnp.bfloat16)
+        spread = dot(jnp.concatenate([high, low], axis=1), double)
+        return (centered * lax.rsqrt(spread + EPSILON) * in_gain[...]).astype(jnp.bfloat16)
+
+    def gated(gates, values):
+        return (0.5 * half_sigmoid(gates) * values).reshape(batch, tokens, channels)
+
+    def project(read, with_right):
+        def step(n, _):
+            some = pl.ds(n * batch, batch)
+            normed = normed_of(read(some).reshape(batch * tokens, channels))
+            a = dot(normed, w_in[:, : 2 * channels])
+            values = gated(a[:, :channels], a[:, channels:])
+            left[some] = values.astype(jnp.bfloat16).astype(jnp.float32)
+            if with_right:
+                b = dot(normed, w_in[:, 2 * channels :])
+                values = gated(b[:, :channels], b[:, channels:]) * token_mask[...]
+                for i in range(batch):
+                    row = values[i] * token_mask[pl.ds(own + n * batch + i, 1), :]
+                    right[n * batch + i] = row.astype(jnp.bfloat16).astype(jnp.float32)
+            return 0
+
+        lax.fori_loop(0, rows // batch, step, 0)
 
     def process(read, owner):
-        def make_left(i, _):
-            normed = normalize(read(i).astype(jnp.float32), in_gain[...]).astype(jnp.bfloat16)
-            values = jax.nn.sigmoid(dot(normed, w_a_gate[...])) * dot(normed, w_a_proj[...])
-            left[i] = values.astype(jnp.bfloat16).astype(jnp.float32)
-            return 0
-
-        lax.fori_loop(0, rows, make_left, 0)
         first = pl.multiple_of(owner * rows, rows)
 
         def tile(t, _):
@@ -164,7 +214,12 @@
         new = old + (gating * update).reshape(rows, rows, channels)
         out[pl.ds(first, rows)] = new.astype(jnp.bfloat16)
 
-    process(lambda *index: pair[index], me)
+    def own_rows(*index):
+        return own_pair[index]
+
+    project(own_rows, True)
+
+    process(own_rows, me)
 
     def arrival(slot, chunk):
         piece = pl.ds(chunk * part, part)
@@ -206,7 +261,11 @@
             for c in range(half):
                 arrival(1 - odd, (1 - odd) * half + c).wait_recv()
 
-        process(lambda *index: halo[(slot,) + index], lax.rem(me + 1 + slot, blocks))
+        def halo_rows(*index):
+            return halo[(slot,) + index]
+
+        project(halo_rows, False)
+        process(halo_rows, lax.rem(me + 1 + slot, blocks))
         return 0
 
     lax.fori_loop(0, 2, halo_step, 0)
@@ -236,13 +295,22 @@
 def shards(blocks, pair, residue_mask, ln_in_gain, *rest):
     w_a_gate, w_a_proj, w_b_gate, w_b_proj, w_out_gate, ln_out_gain, w_out = rest
     rows, tokens, channels = pair.shape
-    vmem = pl.BlockSpec(memory_space=pltpu.VMEM)
+    weight = pltpu.VMEM((channels, channels), jnp.bfloat16)
+    gain = pltpu.VMEM((1, channels), jnp.float32)
     return pl.pallas_call(
         functools.partial(kernel, blocks),
         out_shape=jax.ShapeDtypeStruct((tokens, rows, channels), jnp.bfloat16),
-        in_specs=[vmem] * 10,
-        out_specs=vmem,
+        in_specs=[pl.BlockSpec(memory_space=pltpu.HBM)] * 10,
+        out_specs=pl.BlockSpec(memory_space=pltpu.VMEM),
         scratch_shapes=[
+            pltpu.VMEM((rows, tokens, channels), jnp.bfloat16),
+            pltpu.VMEM((1, tokens), jnp.int32),
+            gain,
+            pltpu.VMEM((channels, 4 * channels), jnp.bfloat16),
+            weight,
+            gain,
+            weight,
+            pltpu.SemaphoreType.DMA((10,)),
             pltpu.VMEM((2, rows, tokens, channels), jnp.bfloat16),
             pltpu.VMEM((rows, tokens, channels), jnp.float32),
             pltpu.VMEM((rows, tokens, channels), jnp.float32),
@@ -255,7 +323,7 @@
             pltpu.SemaphoreType.DMA((blocks,)),
         ],
         compiler_params=pltpu.CompilerParams(
-            collective_id=0, has_side_effects=True, vmem_limit_bytes=48 * 2**20
+            collective_id=0, has_side_effects=True, vmem_limit_bytes=LIMIT
         ),
     )(
         pair,

time: 66.4 us -> 56.9 us (0.86)
  local copies, waits for them, and re-layouts: 7.43 us -> 2.37 us
  Pallas kernels: 58.4 us -> 54.3 us
    unnamed x21 -> x1, local copies, waits for them, and re-layouts: 7.43 us -> 2.37 us
    pallas_call x1, Pallas kernels: 58.4 us -> 54.3 us  [shards(): pl.pallas_call(functools.partial(kernel, blocks), out_shape=jax.ShapeDtyp...]
where the time goes in v2:
time: 56.9 us; the launch traced here: 56.7 us
  Pallas kernels  54.3 us (95%)
  local copies, waits for them, and re-layouts  2.37 us (4%)
    pallas_call x1, Pallas kernels, shards(): pl.pallas_call(functools.partial(kernel, blocks), out_shape=jax.ShapeDtyp...  54.3 us
    unnamed x1, local copies, waits for them, and re-layouts  2.37 us

profile of v2, /device:TPU:15, one launch (start us, length us, event | category | flops | bytes accessed | tf_op | source)
XLA Modules:
  0.0 56.7 jit_solution(2670257706670931852)
XLA Ops:
  0.0 54.3 %shard_map.100 = bf16[256,16,128]{2,1,0:T(8,128)(2,1)} custom-call(bf16[16,256,128]{2,1,0:T(8,128)(2,1)} %pair.1, s32[1,256]{1,0:T(1,128)} %bitcast.3, f32[1,128]{1,0:T(1,128)} %bitcast.4, bf16[128,128]{1,0:T(8,128)(2,1)} %w_a_gate.1, bf16[128,128]{1,0:T(8,128)(2,1)} %w_a_proj.1, bf16[128,128]{1,0:T(8,128)(2,1)} %w_b_gate.1, bf16[128,128]{1,0:T(8,128)(2,1)} %w_b_proj.1, ...), custom_call_target="tpu_custom_call" | custom-call | tf_op jit(solution)/shard_map/pallas_call | solution.py:300
  54.3 2.4 %copy.12 = bf16[256,16,128]{2,1,0:T(8,128)(2,1)} copy(bf16[256,16,128]{2,1,0:T(8,128)(2,1)} %shard_map.100) | data formatting | bytes 2097152

commit v3 on v2

--- a/solution.py
+++ b/solution.py
@@ -53,6 +53,7 @@
     load,
     halo,
     left,
+    kept,
     right,
     product,
     token_mask,
@@ -146,7 +147,7 @@
         copy.wait()
     token_mask[...] = jnp.broadcast_to(mask[...].astype(jnp.float32), (channels, tokens)).T
 
-    batch = max(1, GROUP // tokens)
+    batch = min(part, max(1, GROUP // tokens))
 
     def normed_of(values):
         single = jnp.full((channels, channels), 1.0 / channels, jnp.bfloat16)
@@ -161,25 +162,25 @@
     def gated(gates, values):
         return (0.5 * half_sigmoid(gates) * values).reshape(batch, tokens, channels)
 
-    def project(read, with_right):
-        def step(n, _):
-            some = pl.ds(n * batch, batch)
+    pairs = part * rows
+
+    def work(read, chunk, with_right):
+        for n in range(part // batch):
+            some = pl.ds(chunk * part + n * batch, batch)
             normed = normed_of(read(some).reshape(batch * tokens, channels))
             a = dot(normed, w_in[:, : 2 * channels])
             values = gated(a[:, :channels], a[:, channels:])
-            left[some] = values.astype(jnp.bfloat16).astype(jnp.float32)
+            left[pl.ds(n * batch, batch)] = values.astype(jnp.bfloat16).astype(jnp.float32)
             if with_right:
                 b = dot(normed, w_in[:, 2 * channels :])
                 values = gated(b[:, :channels], b[:, channels:]) * token_mask[...]
                 for i in range(batch):
-                    row = values[i] * token_mask[pl.ds(own + n * batch + i, 1), :]
-                    right[n * batch + i] = row.astype(jnp.bfloat16).astype(jnp.float32)
-            return 0
-
-        lax.fori_loop(0, rows // batch, step, 0)
-
-    def process(read, owner):
-        first = pl.multiple_of(owner * rows, rows)
+                    at_row = chunk * part + n * batch + i
+                    row = values[i] * token_mask[pl.ds(own + at_row, 1), :]
+                    right[at_row] = row.astype(jnp.bfloat16).astype(jnp.float32)
+
+    def combine(read, chunk, owner):
+        first = pl.multiple_of(owner * rows, rows) + chunk * part
 
         def tile(t, _):
             i = (t // (rows // 8)) * 2
@@ -205,21 +206,31 @@
                 product[i + a, pl.ds(j, 8), :] = joined * token_mask[pl.ds(first + i + a, 1), :]
             return 0
 
-        lax.fori_loop(0, (rows // 2) * (rows // 8), tile, 0)
+        lax.fori_loop(0, (part // 2) * (rows // 8), tile, 0)
         normed_x = normalize(product[...], out_gain[...]).astype(jnp.bfloat16)
-        update = dot(normed_x.reshape(rows * rows, channels), w_out[...])
-        old = read(slice(None), pl.ds(own, rows)).astype(jnp.float32)
-        normed = normalize(old, in_gain[...]).astype(jnp.bfloat16)
-        gating = jax.nn.sigmoid(dot(normed.reshape(rows * rows, channels), w_out_gate[...]))
-        new = old + (gating * update).reshape(rows, rows, channels)
-        out[pl.ds(first, rows)] = new.astype(jnp.bfloat16)
+        update = dot(normed_x.reshape(pairs, channels), w_out[...])
+        old = read(pl.ds(chunk * part, part), pl.ds(own, rows))
+        normed = normed_of(old.reshape(pairs, channels))
+        gating = jax.nn.sigmoid(dot(normed, w_out_gate[...]))
+        new = old.astype(jnp.float32) + (gating * update).reshape(part, rows, channels)
+        out[pl.ds(first, part)] = new.astype(jnp.bfloat16)
 
     def own_rows(*index):
         return own_pair[index]
 
-    project(own_rows, True)
-
-    process(own_rows, me)
+    def own_right(chunk, _):
+        work(own_rows, chunk, True)
+        kept[pl.ds(chunk * part, part)] = left[...]
+        return 0
+
+    lax.fori_loop(0, CHUNKS, own_right, 0)
+
+    def own_chunk(chunk, _):
+        left[...] = kept[pl.ds(chunk * part, part)]
+        combine(own_rows, chunk, me)
+        return 0
+
+    lax.fori_loop(0, CHUNKS, own_chunk, 0)
 
     def arrival(slot, chunk):
         piece = pl.ds(chunk * part, part)
@@ -244,31 +255,28 @@
             device_id_type=MESH,
         )
 
-    for c in range(half):
-        arrival(1 - odd, odd * half + c).wait_recv()
-        forward(c).start()
-
-    def halo_step(step, _):
-        slot = lax.rem(odd + step, 2)
-
-        @pl.when(step == 0)
-        def _():
-            for chunk in range(CHUNKS):
-                arrival(odd, chunk).wait_recv()
-
-        @pl.when(step == 1)
+    def halo_step(u, _):
+        slot = (1 - odd) * (u // 4) + odd * (1 - (u // 2) % 2)
+        chunk = (1 - odd) * (u % 4) + odd * (2 * (u // 4) + u % 2)
+
+        @pl.when(u == 4 * odd)
         def _():
             for c in range(half):
-                arrival(1 - odd, (1 - odd) * half + c).wait_recv()
+                arrival(1 - odd, odd * half + c).wait_recv()
+                forward(c).start()
+
+        @pl.when(jnp.logical_or(slot == odd, chunk // half != odd))
+        def _():
+            arrival(slot, chunk).wait_recv()
 
         def halo_rows(*index):
             return halo[(slot,) + index]
 
-        project(halo_rows, False)
-        process(halo_rows, lax.rem(me + 1 + slot, blocks))
-        return 0
-
-    lax.fori_loop(0, 2, halo_step, 0)
+        work(halo_rows, chunk, False)
+        combine(halo_rows, chunk, lax.rem(me + 1 + slot, blocks))
+        return 0
+
+    lax.fori_loop(0, 2 * CHUNKS, halo_step, 0)
 
     for c in range(half):
         forward(c).wait_send()
@@ -312,9 +320,10 @@
             weight,
             pltpu.SemaphoreType.DMA((10,)),
             pltpu.VMEM((2, rows, tokens, channels), jnp.bfloat16),
+            pltpu.VMEM((rows // CHUNKS, tokens, channels), jnp.float32),
             pltpu.VMEM((rows, tokens, channels), jnp.float32),
             pltpu.VMEM((rows, tokens, channels), jnp.float32),
-            pltpu.VMEM((rows, rows, channels), jnp.float32),
+            pltpu.VMEM((rows // CHUNKS, rows, channels), jnp.float32),
             pltpu.VMEM((tokens, channels), jnp.float32),
             pltpu.SemaphoreType.DMA((2, CHUNKS)),
             pltpu.SemaphoreType.DMA((2, CHUNKS)),

time: 56.9 us -> 52.2 us (0.917)
  Pallas kernels: 54.3 us -> 49.7 us
    pallas_call x1, Pallas kernels: 54.3 us -> 49.7 us  [shards(): pl.pallas_call(functools.partial(kernel, blocks), out_shape=jax.ShapeDtyp...]
where the time goes in v3:
time: 52.2 us; the launch traced here: 52 us
  Pallas kernels  49.7 us (95%)
  local copies, waits for them, and re-layouts  2.37 us (5%)
    pallas_call x1, Pallas kernels, shards(): pl.pallas_call(functools.partial(kernel, blocks), out_shape=jax.ShapeDtyp...  49.7 us
    unnamed x1, local copies, waits for them, and re-layouts  2.37 us

profile of v3, /device:TPU:15, one launch (start us, length us, event | category | flops | bytes accessed | tf_op | source)
XLA Modules:
  0.0 52.0 jit_solution(4879652106414133154)
XLA Ops:
  0.0 49.7 %shard_map.100 = bf16[256,16,128]{2,1,0:T(8,128)(2,1)} custom-call(bf16[16,256,128]{2,1,0:T(8,128)(2,1)} %pair.1, s32[1,256]{1,0:T(1,128)} %bitcast.3, f32[1,128]{1,0:T(1,128)} %bitcast.4, bf16[128,128]{1,0:T(8,128)(2,1)} %w_a_gate.1, bf16[128,128]{1,0:T(8,128)(2,1)} %w_a_proj.1, bf16[128,128]{1,0:T(8,128)(2,1)} %w_b_gate.1, bf16[128,128]{1,0:T(8,128)(2,1)} %w_b_proj.1, ...), custom_call_target="tpu_custom_call" | custom-call | tf_op jit(solution)/shard_map/pallas_call | solution.py:308
  49.7 2.4 %copy.12 = bf16[256,16,128]{2,1,0:T(8,128)(2,1)} copy(bf16[256,16,128]{2,1,0:T(8,128)(2,1)} %shard_map.100) | data formatting | bytes 2097152

commit v4 on v3

--- a/solution.py
+++ b/solution.py
@@ -10,8 +10,9 @@
 EPSILON = 1e-05
 MESH = pl.DeviceIdType.MESH
 CHUNKS = 4
-STEPS = 4
+STEPS = 8
 GROUP = 1024
+FIRST = 1
 LIMIT = 63 * 2**20
 
 
@@ -52,6 +53,7 @@
     w_out,
     load,
     halo,
+    relay,
     left,
     kept,
     right,
@@ -62,6 +64,8 @@
     forward_send,
     block_send,
     block_recv,
+    relay_send,
+    relay_recv,
 ):
     rows, tokens, channels = pair.shape
     me = lax.axis_index("row")
@@ -137,11 +141,63 @@
             device_id_type=MESH,
         )
 
+    def relayed(source, distance):
+        chip = source // 2
+        target_chip = lax.rem(source + distance, blocks) // 2
+        across = jnp.logical_and(lax.rem(chip, 2) == 0, lax.rem(target_chip, 2) == 1)
+        return jnp.logical_and(across, target_chip != chip + 1)
+
+    def to_relay(distance, source, device):
+        target = lax.rem(source + distance, blocks)
+        columns = pl.ds(pl.multiple_of(target * rows, rows), rows)
+        return pltpu.make_async_remote_copy(
+            src_ref=pair.at[:, columns],
+            dst_ref=relay.at[distance],
+            send_sem=block_send.at[distance],
+            recv_sem=relay_recv.at[distance],
+            device_id={"row": device},
+            device_id_type=MESH,
+        )
+
+    before = lax.rem(me + blocks - 2, blocks)
+    after = lax.rem(me + 2, blocks)
+
+    def from_relay(distance):
+        return pltpu.make_async_remote_copy(
+            src_ref=relay.at[distance],
+            dst_ref=out.at[pl.ds(pl.multiple_of(before * rows, rows), rows)],
+            send_sem=relay_send.at[distance],
+            recv_sem=block_recv.at[distance],
+            device_id={"row": lax.rem(before + distance, blocks)},
+            device_id_type=MESH,
+        )
+
+    def send_relayed(distance, _):
+        @pl.when(relayed(me, distance))
+        def _():
+            to_relay(distance, me, after).start()
+
+        return 0
+
     def send_block(distance, _):
-        block_copy(distance).start()
-        return 0
-
+        @pl.when(jnp.logical_not(relayed(me, distance)))
+        def _():
+            block_copy(distance).start()
+
+        return 0
+
+    lax.fori_loop(1, blocks - 2, send_relayed, 0)
     lax.fori_loop(1, blocks - 2, send_block, 0)
+
+    def pass_on(distance, _):
+        @pl.when(relayed(before, distance))
+        def _():
+            to_relay(distance, before, before).wait_recv()
+            from_relay(distance).start()
+
+        return 0
+
+    share = -(-(blocks - 3) // (2 * CHUNKS - FIRST))
 
     for copy in loads:
         copy.wait()
@@ -269,6 +325,10 @@
         def _():
             arrival(slot, chunk).wait_recv()
 
+        lower = jnp.minimum(1 + jnp.maximum(u - FIRST, 0) * share, blocks - 2)
+        upper = jnp.minimum(1 + jnp.maximum(u + 1 - FIRST, 0) * share, blocks - 2)
+        lax.fori_loop(lower, upper, pass_on, 0)
+
         def halo_rows(*index):
             return halo[(slot,) + index]
 
@@ -295,6 +355,11 @@
         )
         landed.wait_recv()
         block_copy(distance).wait_send()
+
+        @pl.when(relayed(before, distance))
+        def _():
+            from_relay(distance).wait_send()
+
         return 0
 
     lax.fori_loop(1, blocks - 2, finish_block, 0)
@@ -320,6 +385,7 @@
             weight,
             pltpu.SemaphoreType.DMA((10,)),
             pltpu.VMEM((2, rows, tokens, channels), jnp.bfloat16),
+            pltpu.VMEM((blocks, rows, rows, channels), jnp.bfloat16),
             pltpu.VMEM((rows // CHUNKS, tokens, channels), jnp.float32),
             pltpu.VMEM((rows, tokens, channels), jnp.float32),
             pltpu.VMEM((rows, tokens, channels), jnp.float32),
@@ -328,6 +394,8 @@
             pltpu.SemaphoreType.DMA((2, CHUNKS)),
             pltpu.SemaphoreType.DMA((2, CHUNKS)),
             pltpu.SemaphoreType.DMA((CHUNKS // 2,)),
+            pltpu.SemaphoreType.DMA((blocks,)),
+            pltpu.SemaphoreType.DMA((blocks,)),
             pltpu.SemaphoreType.DMA((blocks,)),
             pltpu.SemaphoreType.DMA((blocks,)),
         ],

time: 52.2 us -> 51.4 us (0.985)
  the two profiles are of different devices: /device:TPU:15 before, /device:TPU:1 now
where the time goes in v4:
time: 51.4 us; the launch traced here: 51.2 us
  Pallas kernels  48.9 us (95%)
  local copies, waits for them, and re-layouts  2.37 us (5%)
    pallas_call x1, Pallas kernels, shards(): pl.pallas_call(functools.partial(kernel, blocks), out_shape=jax.ShapeDtyp...  48.9 us
    unnamed x1, local copies, waits for them, and re-layouts  2.37 us

profile of v4, /device:TPU:1, one launch (start us, length us, event | category | flops | bytes accessed | tf_op | source)
XLA Modules:
  0.0 51.2 jit_solution(9066260469635851833)
XLA Ops:
  0.0 48.9 %shard_map.100 = bf16[256,16,128]{2,1,0:T(8,128)(2,1)} custom-call(bf16[16,256,128]{2,1,0:T(8,128)(2,1)} %pair.1, s32[1,256]{1,0:T(1,128)} %bitcast.3, f32[1,128]{1,0:T(1,128)} %bitcast.4, bf16[128,128]{1,0:T(8,128)(2,1)} %w_a_gate.1, bf16[128,128]{1,0:T(8,128)(2,1)} %w_a_proj.1, bf16[128,128]{1,0:T(8,128)(2,1)} %w_b_gate.1, bf16[128,128]{1,0:T(8,128)(2,1)} %w_b_proj.1, ...), custom_call_target="tpu_custom_call" | custom-call | tf_op jit(solution)/shard_map/pallas_call | solution.py:373
  48.9 2.4 %copy.12 = bf16[256,16,128]{2,1,0:T(8,128)(2,1)} copy(bf16[256,16,128]{2,1,0:T(8,128)(2,1)} %shard_map.100) | data formatting | bytes 2097152
